TPU v7x, 32 devices: a whole 2x2x4 slice. The times are simulated.
32 devices in a mesh: dp: 8 (over z, y), tensor: 4 (over x, core).
Axes of the slice: x: 2, y: 2, z: 4, core: 2. Of those that a mesh axis runs over, the one named last changes fastest.
Arguments:
- context: bfloat16 [4096, 1024], P('dp', 'tensor'), may hold values from -6 to 6
- w_out: bfloat16 [1024, 4096], P('tensor'), may hold values from -0.375 to 0.375
- encoder: bfloat16 [4096, 512], replicated, may hold values from -0.09375 to 0.09375
- decoder: bfloat16 [2048, 4096], P(None, 'tensor'), may hold values from -0.125 to 0.125
- out_grad: bfloat16 [4096, 4096], P('dp', 'tensor'), may hold values from -6 to 6
Outputs:
- mixed: bfloat16 [4096, 4096], P('dp', 'tensor')
- grad_context: bfloat16 [4096, 1024], P('dp', 'tensor')
- grad_wout: float32 [4096, 1024], P('dp', 'tensor')
All inputs are finite; a program needn't handle non-finite values.
Results may differ from a plain program's by a relative error of at most 0.0057.
Values may be sent and summed in bfloat16 or wider, within the bound.
A program may use at most 128 MiB of HBM per device.

v0:
```python
import jax
import jax.numpy as jnp
from jax import lax
from jax.sharding import PartitionSpec as P


def on_device(context, w_out, encoder, decoder, out_grad):
    partial_value = jnp.dot(context, w_out, preferred_element_type=jnp.float32).astype(jnp.bfloat16)
    code = jnp.dot(partial_value, encoder, preferred_element_type=jnp.float32).astype(jnp.bfloat16)
    rows = decoder
    mixed = jnp.dot(
        lax.all_gather(code, "tensor", axis=1, tiled=True), rows, preferred_element_type=jnp.float32
    ).astype(jnp.bfloat16)
    rows = decoder
    grad_codes = lax.psum_scatter(
        lax.dot_general(
            rows, out_grad, (((1,), (1,)), ((), ())), preferred_element_type=jnp.float32
        ),
        "tensor",
        scatter_dimension=0,
        tiled=True,
    ).astype(jnp.bfloat16)
    part_grad = lax.dot_general(
        grad_codes, encoder, (((0,), (1,)), ((), ())), preferred_element_type=jnp.float32
    ).astype(jnp.bfloat16)
    grad_context = lax.dot_general(
        part_grad, w_out, (((1,), (1,)), ((), ())), preferred_element_type=jnp.float32
    ).astype(jnp.bfloat16)
    replicas = lax.axis_size("dp")
    summed = lax.psum_scatter(
        lax.dot_general(
            part_grad, context, (((0,), (0,)), ((), ())), preferred_element_type=jnp.float32
        ),
        "dp",
        scatter_dimension=0,
        tiled=True,
    )
    grad_wout = summed / replicas
    return (mixed, grad_context, grad_wout)


def solution(mesh):
    in_specs = (P("dp", "tensor"), P("tensor", None), P(), P(None, "tensor"), P("dp", "tensor"))
    out_specs = (P("dp", "tensor"), P("dp", "tensor"), P("dp", "tensor"))
    return jax.shard_map(
        on_device, mesh=mesh, in_specs=in_specs, out_specs=out_specs, check_vma=False
    )
```

profile of v0, /device:TPU:0, one launch (start us, length us, event | category | flops | bytes accessed | tf_op | source)
XLA Modules:
  0.0 186.8 jit_solution(5072054783811373776)
XLA Ops:
  7.2 0.0 copy-start
  7.2 0.0 reduce-scatter.3.cloned.1.call-start
  7.2 7.0 %fusion.3 = f32[2048,512]{1,0:T(8,128)} fusion(bf16[2048,1024]{1,0:T(8,128)(2,1)} %param.8, bf16[512,1024]{1,0:T(8,128)(2,1)} %param.9), kind=kOutput, calls=%fused_computation.8 | convolution fusion | flops 2147483648 | bytes 9437184 | tf_op jit(solution)/shard_map/dot_general | solution.py:16
  14.2 0.0 copy-start.3
  14.2 0.0 reduce-scatter.3.cloned.1.call-update
  14.2 0.0 all-gather.2.cloned.1.call-start
  14.3 0.0 copy-done
  14.3 0.9 copy-done.3
  15.1 6.4 %fusion.1 = bf16[512,512]{1,0:T(8,128)(2,1)} fusion(bf16[4096,512]{1,0:T(8,128)(2,1)} %param.7, bf16[512,256]{1,0:T(8,128)(2,1)S(1)} %copy-done.3, bf16[256,4096]{1,0:T(8,128)(2,1)S(1)} %copy-done), kind=kOutput, calls=%fused_computation.4 | convolution fusion | flops 3223584768 | bytes 7077888 | tf_op jit(solution)/shard_map/dot_general | solution.py:9
  21.5 0.0 all-gather.2.cloned.1.call-update
  21.6 0.0 reduce-scatter.5.cloned.1.call-start
  21.6 40.0 %reduce-scatter.3.cloned.1.call-done = f32[512,512]{1,0:T(8,128)} async-done(((f32[2048,512]{1,0:T(8,128)}), f32[512,512]{1,0:T(8,128)}) %reduce-scatter.3.cloned.1.call-update) | async-done | bytes 1048592 | tf_op jit(solution)/shard_map/reduce_scatter | solution.py:15
  61.6 4.9 %convolution_convert_fusion.1 = bf16[512,4096]{1,0:T(8,128)(2,1)S(1)} fusion(bf16[4096,512]{1,0:T(8,128)(2,1)} %param.7, f32[512,512]{1,0:T(8,128)} %reduce-scatter.3.cloned.1.call-done), kind=kOutput, calls=%fused_computation.1 | convolution fusion | flops 2149842944 | bytes 9437184 | tf_op jit(solution)/shard_map/dot_general | solution.py:23
  66.5 0.0 copy-start.1
  66.5 1.9 %copy-done.1 = bf16[512,4096]{1,0:T(8,128)(2,1)} copy-done((bf16[512,4096]{1,0:T(8,128)(2,1)}, bf16[512,4096]{1,0:T(8,128)(2,1)S(1)}, u32[]{:S(2)}) %copy-start.1) | copy-done | bytes 4194328
  68.4 3.3 %fusion.4 = f32[4096,256]{1,0:T(8,128)} fusion(bf16[512,4096]{1,0:T(8,128)(2,1)S(1)} %convolution_convert_fusion.1, bf16[512,256]{1,0:T(8,128)(2,1)S(1)} %copy-done.3), kind=kOutput, calls=%fused_computation.9 | convolution fusion | flops 1073741824 | bytes 8650752 | tf_op jit(solution)/shard_map/dot_general | solution.py:31
  71.7 0.0 reduce-scatter.5.cloned.1.call-update
  71.7 14.7 %all-gather.2.cloned.1.call-done = bf16[512,2048]{1,0:T(8,128)(2,1)} async-done(((bf16[512,512]{1,0:T(8,128)(2,1)}), bf16[512,2048]{1,0:T(8,128)(2,1)}) %all-gather.2.cloned.1.call-update) | async-done | bytes 2097168 | tf_op jit(solution)/shard_map/all_gather | solution.py:12
  86.4 0.0 copy-start.2
  86.4 6.3 %convolution_convert_fusion.2 = bf16[512,1024]{1,0:T(8,128)(2,1)} fusion(bf16[512,2048]{1,0:T(8,128)(2,1)} %all-gather.2.cloned.1.call-done, bf16[2048,1024]{1,0:T(8,128)(2,1)} %param.8), kind=kOutput, calls=%fused_computation.3 | convolution fusion | flops 2148007936 | bytes 7340032 | tf_op jit(solution)/shard_map/dot_general | solution.py:11
  92.7 0.0 copy-done.2
  92.7 2.0 %convolution_convert_fusion.3 = bf16[512,256]{1,0:T(8,128)(2,1)} fusion(bf16[512,4096]{1,0:T(8,128)(2,1)S(1)} %copy-done.2, bf16[256,4096]{1,0:T(8,128)(2,1)S(1)} %copy-done), kind=kOutput, calls=%fused_computation.5 | convolution fusion | flops 1073872896 | bytes 6553600 | tf_op jit(solution)/shard_map/dot_general | solution.py:26
  94.7 83.7 %reduce-scatter.5.cloned.1.call-done = f32[512,256]{1,0:T(8,128)} async-done(((f32[4096,256]{1,0:T(8,128)}), f32[512,256]{1,0:T(8,128)}) %reduce-scatter.5.cloned.1.call-update) | async-done | bytes 524304 | tf_op jit(solution)/shard_map/reduce_scatter | solution.py:30
  178.4 1.9 %broadcast_multiply_fusion = f32[512,256]{1,0:T(8,128)} fusion(f32[512,256]{1,0:T(8,128)} %reduce-scatter.5.cloned.1.call-done), kind=kLoop, calls=%fused_computation.7 | loop fusion | flops 131072 | bytes 1048576 | tf_op jit(solution)/shard_map/div | solution.py:38
Async XLA Ops:
  7.2 7.1 %copy-start = (bf16[256,4096]{1,0:T(8,128)(2,1)S(1)}, bf16[256,4096]{1,0:T(8,128)(2,1)}, u32[]{:S(2)}) copy-start(bf16[256,4096]{1,0:T(8,128)(2,1)} %param.6) | copy-start | bytes 6291460
  7.2 54.4 %reduce-scatter.3.cloned.1.call-start = ((), (), s32[]{:S(2)}) async-start(), calls=%async_computation.3 | async-start | bytes 5242880 | tf_op jit(solution)/shard_map/reduce_scatter | solution.py:15
  14.2 0.9 copy-start.3
  14.2 72.2 %all-gather.2.cloned.1.call-start = ((), (), s32[]{:S(2)}) async-start(), calls=%async_computation.2 | async-start | bytes 2621440 | tf_op jit(solution)/shard_map/all_gather | solution.py:12
  21.6 156.9 %reduce-scatter.5.cloned.1.call-start = ((), (), s32[]{:S(2)}) async-start(), calls=%async_computation.4 | async-start | bytes 4718592 | tf_op jit(solution)/shard_map/reduce_scatter | solution.py:30
  66.5 1.9 %copy-start.1 = (bf16[512,4096]{1,0:T(8,128)(2,1)}, bf16[512,4096]{1,0:T(8,128)(2,1)S(1)}, u32[]{:S(2)}) copy-start(bf16[512,4096]{1,0:T(8,128)(2,1)S(1)} %convolution_convert_fusion.1) | copy-start | bytes 12582916
  86.4 6.3 %copy-start.2 = (bf16[512,4096]{1,0:T(8,128)(2,1)S(1)}, bf16[512,4096]{1,0:T(8,128)(2,1)}, u32[]{:S(2)}) copy-start(bf16[512,4096]{1,0:T(8,128)(2,1)} %copy-done.1) | copy-start | bytes 12582916
Sparse Core Ops, SparseCore 0:
  14.3 47.1 reduce-scatter.2
  63.8 22.5 all-gather.1
  90.5 87.8 reduce-scatter.4
where the time goes:
time: 187 us
  waiting for transfers between devices  138 us (74%)
  matrix products  29.8 us (16%)
  between operations  13.8 us (7%)
  local copies, waits for them, and re-layouts  2.81 us (2%)
  other arithmetic  1.87 us (1%)
    reduce_scatter x1, waiting for transfers between devices, on_device(): lax.psum_scatter(lax.dot_general(part_grad, context, (((0,), (0,)), ((),...  83.7 us
    reduce_scatter x1, waiting for transfers between devices, on_device(): lax.psum_scatter(lax.dot_general(rows, out_grad, (((1,), (1,)), ((), ()))...  40 us
    all_gather x1, waiting for transfers between devices, on_device(): lax.all_gather(code, 'tensor', axis=1, tiled=True)  14.7 us
    dot_general x1, matrix products, on_device(): lax.dot_general(rows, out_grad, (((1,), (1,)), ((), ())), preferred_eleme...  6.95 us
    dot_general x1, matrix products, on_device(): jnp.dot(partial_value, encoder, preferred_element_type=jnp.float32)  6.4 us
    dot_general x1, matrix products, on_device(): jnp.dot(lax.all_gather(code, 'tensor', axis=1, tiled=True), rows, preferr...  6.27 us
    dot_general x1, matrix products, on_device(): lax.dot_general(grad_codes, encoder, (((0,), (1,)), ((), ())), preferred_...  4.91 us
  transfers between devices with their start and end apart: 3, of which 3 were waited for; matrix products, arithmetic and copies ran while one was open for 12% of the time, Pallas kernels for 0%

commit v1 on v0

v1 whole, which is shorter than its diff:
```python
import jax
import jax.numpy as jnp
from jax import lax
from jax.sharding import PartitionSpec as P


def dot(a, b, ca, cb):
    return lax.dot_general(a, b, (((ca,), (cb,)), ((), ())), preferred_element_type=jnp.float32)


def on_device(context, w_out, encoder, decoder, out_grad):
    replicas = lax.axis_size("dp")
    own_rows = encoder.shape[0] // replicas
    product = dot(w_out, encoder, 1, 0).astype(jnp.bfloat16)
    code = dot(context, product, 1, 0).astype(jnp.bfloat16)
    mixed = dot(lax.all_gather(code, "tensor", axis=1, tiled=True), decoder, 1, 0).astype(jnp.bfloat16)
    grad_codes = lax.psum_scatter(
        dot(decoder, out_grad, 1, 1), "tensor", scatter_dimension=0, tiled=True
    ).astype(jnp.bfloat16)
    grad_context = dot(grad_codes, product, 0, 1).astype(jnp.bfloat16)
    inner = lax.psum(dot(grad_codes, context, 1, 0), "dp").astype(jnp.bfloat16)
    rows = lax.dynamic_slice_in_dim(encoder, lax.axis_index("dp") * own_rows, own_rows, 0)
    grad_wout = dot(rows, inner, 1, 0) / replicas
    return (mixed, grad_context, grad_wout)


def solution(mesh):
    in_specs = (P("dp", "tensor"), P("tensor", None), P(), P(None, "tensor"), P("dp", "tensor"))
    out_specs = (P("dp", "tensor"), P("dp", "tensor"), P("dp", "tensor"))
    return jax.shard_map(
        on_device, mesh=mesh, in_specs=in_specs, out_specs=out_specs, check_vma=False
    )
```

time: 187 us -> 144 us (0.77)
  waiting for transfers between devices: 138 us -> 59.8 us
  blocking collectives: 0 us -> 44.1 us
  matrix products: 29.8 us -> 23.8 us
  other arithmetic: 1.87 us -> 0 us
    reduce_scatter x2 -> x1, waiting for transfers between devices: 124 us -> 40.9 us  [on_device(): lax.psum_scatter(dot(decoder, out_grad, 1, 1), 'tensor', scatter_dimensio...]
    psum x0 -> x1, blocking collectives: none -> 44.1 us  [on_device(): inner = lax.psum(dot(grad_codes, context, 1, 0), 'dp').astype(jnp.bfloat16)]
    dot_general x6 -> x7, matrix products: 29.8 us -> 23.8 us  [dot(): lax.dot_general(a, b, (((ca,), (cb,)), ((), ())), preferred_element_type=...]
    all_gather x1, waiting for transfers between devices: 14.7 us -> 18.8 us  [on_device(): lax.all_gather(code, 'tensor', axis=1, tiled=True)]
  transfers between devices with their start and end apart: 3 -> 2, of which waited for: 3 -> 2; matrix products, arithmetic and copies ran while one was open for 12% -> 9% of each run, Pallas kernels for 0% -> 0%
where the time goes in v1:
time: 144 us
  waiting for transfers between devices  59.8 us (42%)
  blocking collectives  44.1 us (31%)
  matrix products  23.8 us (17%)
  between operations  14.1 us (10%)
  local copies, waits for them, and re-layouts  2.23 us (2%)
    psum x1, blocking collectives, on_device(): inner = lax.psum(dot(grad_codes, context, 1, 0), 'dp').astype(jnp.bfloat16)  44.1 us
    reduce_scatter x1, waiting for transfers between devices, on_device(): lax.psum_scatter(dot(decoder, out_grad, 1, 1), 'tensor', scatter_dimensio...  40.9 us
    dot_general x7, matrix products, dot(): lax.dot_general(a, b, (((ca,), (cb,)), ((), ())), preferred_element_type=...  23.8 us
    all_gather x1, waiting for transfers between devices, on_device(): lax.all_gather(code, 'tensor', axis=1, tiled=True)  18.8 us
  transfers between devices with their start and end apart: 2, of which 2 were waited for; matrix products, arithmetic and copies ran while one was open for 9% of the time, Pallas kernels for 0%

profile of v1, /device:TPU:0, one launch (start us, length us, event | category | flops | bytes accessed | tf_op | source)
XLA Modules:
  0.0 144.1 jit_solution(5202912162681319914)
XLA Ops:
  7.2 0.0 copy-start
  7.2 0.0 copy-start.2
  7.2 0.0 copy-start.4
  7.2 0.0 all-gather.2.cloned.1.call-start
  7.2 1.5 %copy-done = bf16[256,4096]{1,0:T(8,128)(2,1)S(1)} copy-done((bf16[256,4096]{1,0:T(8,128)(2,1)S(1)}, bf16[256,4096]{1,0:T(8,128)(2,1)}, u32[]{:S(2)}) %copy-start) | copy-done | bytes 2097176
  8.8 3.4 %convolution_convert_fusion.3 = bf16[256,512]{1,0:T(8,128)(2,1)S(1)} fusion(bf16[256,4096]{1,0:T(8,128)(2,1)S(1)} %copy-done, bf16[4096,512]{1,0:T(8,128)(2,1)} %param.7), kind=kOutput, calls=%fused_computation.5 | convolution fusion | flops 1073872896 | bytes 6553600 | tf_op jit(solution)/shard_map/dot_general | solution.py:8
  12.2 0.0 copy-start.3
  12.2 0.7 copy-done.3
  12.9 0.0 copy-done.2
  12.9 1.1 fusion
  14.0 0.0 all-gather.2.cloned.1.call-update
  14.1 0.0 reduce-scatter.2.cloned.1.call-start
  14.1 0.0 copy-done.4
  14.1 6.5 %fusion.7 = f32[2048,512]{1,0:T(8,128)} fusion(bf16[2048,1024]{1,0:T(8,128)(2,1)} %param.8, bf16[512,1024]{1,0:T(8,128)(2,1)S(1)} %copy-done.4), kind=kOutput, calls=%fused_computation.12 | convolution fusion | flops 2147483648 | bytes 9437184 | tf_op jit(solution)/shard_map/dot_general | solution.py:8
  20.6 0.0 reduce-scatter.2.cloned.1.call-update
  20.7 18.8 %all-gather.2.cloned.1.call-done = bf16[512,2048]{0,1:T(8,128)(2,1)} async-done(((bf16[512,512]{0,1:T(8,128)(2,1)}), bf16[512,2048]{0,1:T(8,128)(2,1)}) %all-gather.2.cloned.1.call-update) | async-done | bytes 2097168 | tf_op jit(solution)/shard_map/all_gather | solution.py:16
  39.5 6.1 %convolution_convert_fusion = bf16[512,1024]{1,0:T(8,128)(2,1)} fusion(bf16[512,2048]{0,1:T(8,128)(2,1)} %all-gather.2.cloned.1.call-done, bf16[2048,1024]{1,0:T(8,128)(2,1)} %param.8), kind=kOutput, calls=%fused_computation | convolution fusion | flops 2148007936 | bytes 7340032 | tf_op jit(solution)/shard_map/dot_general | solution.py:8
  45.6 40.9 %reduce-scatter.2.cloned.1.call-done = f32[512,512]{1,0:T(8,128)} async-done(((f32[2048,512]{1,0:T(8,128)}), f32[512,512]{1,0:T(8,128)}) %reduce-scatter.2.cloned.1.call-update) | async-done | bytes 1048592 | tf_op jit(solution)/shard_map/reduce_scatter | solution.py:17
  86.6 0.0 copy-start.1
  86.6 2.4 %fusion.3 = f32[512,256]{1,0:T(8,128)} fusion(bf16[512,256]{1,0:T(8,128)(2,1)S(1)} %copy-done.2, f32[512,512]{1,0:T(8,128)} %reduce-scatter.2.cloned.1.call-done), kind=kOutput, calls=%fused_computation.8 | convolution fusion | flops 134479872 | bytes 1835008 | tf_op jit(solution)/shard_map/dot_general | solution.py:8
  89.0 44.1 %all-reduce.1 = bf16[512,256]{1,0:T(8,128)(2,1)S(1)} all-reduce(f32[512,256]{1,0:T(8,128)} %fusion.3), channel_id=1, replica_groups=mesh['dp'=8,'tensor'=4] {'dp'}, use_global_device_ids=true, to_apply=%region_1.0 | all-reduce | flops 131072 | bytes 786432 | tf_op jit(solution)/shard_map/psum | solution.py:21
  133.1 2.1 %convolution_multiply_fusion = f32[512,256]{1,0:T(8,128)} fusion(bf16[4096,512]{1,0:T(8,128)(2,1)} %param.7, s32[]{:T(128)S(6)} %select_n.3, bf16[512,256]{1,0:T(8,128)(2,1)S(1)} %all-reduce.1), kind=kOutput, calls=%fused_computation.3 | convolution fusion | flops 134348800 | bytes 1310724 | tf_op jit(solution)/shard_map/dot_general | solution.py:8
  135.3 0.0 copy-done.1
  135.3 2.0 %convolution_convert_fusion.2 = bf16[512,256]{1,0:T(8,128)(2,1)} fusion(bf16[256,512]{1,0:T(8,128)(2,1)} %copy-done.3, f32[512,512]{1,0:T(8,128)S(1)} %copy-done.1), kind=kOutput, calls=%fused_computation.4 | convolution fusion | flops 134610944 | bytes 1572864 | tf_op jit(solution)/shard_map/dot_general | solution.py:8
Async XLA Ops:
  7.2 1.6 %copy-start = (bf16[256,4096]{1,0:T(8,128)(2,1)S(1)}, bf16[256,4096]{1,0:T(8,128)(2,1)}, u32[]{:S(2)}) copy-start(bf16[256,4096]{1,0:T(8,128)(2,1)} %param.6) | copy-start | bytes 6291460
  7.2 5.7 %copy-start.2 = (bf16[512,256]{1,0:T(8,128)(2,1)S(1)}, bf16[512,256]{1,0:T(8,128)(2,1)}, u32[]{:S(2)}) copy-start(bf16[512,256]{1,0:T(8,128)(2,1)} %param.5) | copy-start | bytes 786436
  7.2 6.9 %copy-start.4 = (bf16[512,1024]{1,0:T(8,128)(2,1)S(1)}, bf16[512,1024]{1,0:T(8,128)(2,1)}, u32[]{:S(2)}) copy-start(bf16[512,1024]{1,0:T(8,128)(2,1)} %param.9) | copy-start | bytes 3145732
  7.2 32.3 %all-gather.2.cloned.1.call-start = ((), (), s32[]{:S(2)}) async-start(), calls=%async_computation.1 | async-start | bytes 2621440 | tf_op jit(solution)/shard_map/all_gather | solution.py:16
  12.2 0.7 copy-start.3
  14.1 72.5 %reduce-scatter.2.cloned.1.call-start = ((), (), s32[]{:S(2)}) async-start(), calls=%async_computation.2 | async-start | bytes 5242880 | tf_op jit(solution)/shard_map/reduce_scatter | solution.py:17
  86.6 48.7 %copy-start.1 = (f32[512,512]{1,0:T(8,128)S(1)}, f32[512,512]{1,0:T(8,128)}, u32[]{:S(2)}) copy-start(f32[512,512]{1,0:T(8,128)} %reduce-scatter.2.cloned.1.call-done) | copy-start | bytes 3145732
Sparse Core Ops, SparseCore 0:
  14.2 25.2 all-gather.1
  42.0 44.4 reduce-scatter.1

commit v2 on v1

v2 whole, which is shorter than its diff:
```python
import functools

import jax
import jax.numpy as jnp
from jax import lax
from jax.experimental import pallas as pl
from jax.experimental.pallas import tpu as pltpu
from jax.sharding import PartitionSpec as P

BF16, F32 = jnp.bfloat16, jnp.float32
CHUNKS = 2


def dot(a, b, ca, cb):
    return lax.dot_general(a, b, (((ca,), (cb,)), ((), ())), preferred_element_type=F32)


def kernel(
    S, R,
    ctx_h, w_h, enc_h, dec_h, og_h,
    mixed_h, gctx_h, gw_h,
    ctx, w, enc, dec, og,
    we, codes, pair_out, pair_in, chip_out, chip_in, cg_own, cg,
    gt_own, gt_out, gt_in, gt_all, acc, mixed, gctx, gw,
    load_sem, dec_sem, store_sem, mix_sem,
    pair_ss, pair_rs, chip_ss, chip_rs, near_ss, far_ss, fwd_ss, code_rs,
    sum_ss, sum_rs, all_ss, all_rs,
):
    K = S // 2
    T, HW = ctx.shape
    C = we.shape[1]
    D = enc.shape[0]
    part = HW // R
    own_rows = D // R
    step = T // CHUNKS
    d, t = lax.axis_index("dp"), lax.axis_index("tensor")
    k, c = t // 2, lax.rem(t, 2)
    mate = 2 * k + 1 - c

    def chip(o):
        return lax.rem(k + o, K)

    def rows(ch):
        return pl.ds(pl.multiple_of(ch * step, step), step)

    def block(j):
        return pl.ds(pl.multiple_of(j * C, C), C)

    def piece(r):
        return pl.ds(pl.multiple_of(r * part, part), part)

    def remote(src, dst, ss, rs, **where):
        return pltpu.make_async_remote_copy(
            src_ref=src, dst_ref=dst, send_sem=ss, recv_sem=rs,
            device_id=where, device_id_type=pl.DeviceIdType.MESH,
        )

    def load(i, src, dst):
        return pltpu.make_async_copy(src, dst, load_sem.at[i])

    def load_dec(j):
        return pltpu.make_async_copy(dec_h.at[block(j), :], dec.at[block(j), :], dec_sem.at[j])

    load_og = load(0, og_h, og)
    load_w, load_enc, load_ctx = load(1, w_h, w), load(2, enc_h, enc), load(3, ctx_h, ctx)
    load_og.start()

    @pl.loop(0, K)
    def _(i):
        o = lax.rem(i + 1, K)
        load_dec(2 * chip(o) + 1 - c).start()
        load_dec(2 * chip(o) + c).start()

    load_w.start()
    load_enc.start()
    load_ctx.start()

    barrier = pltpu.get_barrier_semaphore()
    MESH = pl.DeviceIdType.MESH
    pl.semaphore_signal(barrier, inc=1, device_id={"tensor": mate}, device_id_type=MESH)

    @pl.loop(1, K)
    def _(o):
        pl.semaphore_signal(barrier, inc=1, device_id={"tensor": 2 * chip(o) + c}, device_id_type=MESH)

    @pl.loop(1, R)
    def _(o):
        pl.semaphore_signal(barrier, inc=1, device_id={"dp": lax.rem(d + o, R)}, device_id_type=MESH)

    pl.semaphore_wait(barrier, 1 + (K - 1) + (R - 1))

    def pair_copy(o, ch):
        return remote(pair_out.at[o, rows(ch), :], pair_in.at[o, rows(ch), :],
                      pair_ss.at[o, ch], pair_rs.at[o, ch], tensor=mate)

    def chip_copy(o, ch):
        return remote(chip_out.at[o, rows(ch), :], chip_in.at[o, rows(ch), :],
                      chip_ss.at[o, ch], chip_rs.at[o, ch], tensor=2 * chip(o) + c)

    load_og.wait()

    def for_mate(o):
        j = 2 * chip(o) + 1 - c
        load_dec(j).wait()

        @pl.loop(0, CHUNKS)
        def _(ch):
            pair_out[o, rows(ch), :] = dot(og[rows(ch), :], dec[block(j), :], 1, 1).astype(BF16)
            pair_copy(o, ch).start()

    @pl.loop(1, K)
    def _(o):
        for_mate(o)
        j = 2 * chip(o) + c
        load_dec(j).wait()

        @pl.loop(0, CHUNKS)
        def _(ch):
            cg_own[rows(ch), :] = dot(og[rows(ch), :], dec[block(j), :], 1, 1)
            pair_copy(o, ch).wait_recv()
            chip_out[o, rows(ch), :] = (
                cg_own[rows(ch), :] + pair_in[o, rows(ch), :].astype(F32)
            ).astype(BF16)
            chip_copy(o, ch).start()

    for_mate(0)
    load_dec(t).wait()

    @pl.loop(0, CHUNKS)
    def _(ch):
        cg_own[rows(ch), :] = dot(og[rows(ch), :], dec[block(t), :], 1, 1)

    load_w.wait()
    load_enc.wait()
    we[...] = dot(w[...], enc[...], 1, 0).astype(BF16)
    load_ctx.wait()

    def near_copy(j):
        return remote(codes.at[j], codes.at[j], near_ss, code_rs.at[j, 0], tensor=mate)

    def far_copy(j, o, ch):
        return remote(codes.at[j, rows(ch), :], codes.at[j, rows(ch), :],
                      far_ss.at[o, ch], code_rs.at[j, ch], tensor=2 * chip(o) + c)

    def fwd_copy(j, o, ch):
        return remote(codes.at[j, rows(ch), :], codes.at[j, rows(ch), :],
                      fwd_ss.at[o, ch], code_rs.at[j, ch], tensor=mate)

    codes[t] = dot(ctx[...], we[...], 1, 0).astype(BF16)
    near_copy(t).start()

    @pl.loop(0, CHUNKS)
    def _(ch):
        acc[rows(ch), :] = dot(codes[t, rows(ch), :], dec[block(t), :], 1, 0)

    near_copy(mate).wait_recv()

    @pl.loop(0, CHUNKS)
    def _(ch):
        acc[rows(ch), :] += dot(codes[mate, rows(ch), :], dec[block(mate), :], 1, 0)

    @pl.loop(1, K)
    def _(o):
        @pl.loop(0, CHUNKS)
        def _(ch):
            chip_copy(o, ch).wait_send()
            far_copy(t, o, ch).start()

    @pl.loop(0, CHUNKS)
    def _(ch):
        pair_copy(0, ch).wait_recv()
        cg_own[rows(ch), :] += pair_in[0, rows(ch), :].astype(F32)

        @pl.loop(1, K)
        def _(o):
            chip_copy(o, ch).wait_recv()
            cg_own[rows(ch), :] += chip_in[o, rows(ch), :].astype(F32)

        cg[rows(ch), :] = cg_own[rows(ch), :].astype(BF16)

    def sum_copy(o):
        return remote(gt_out.at[piece(lax.rem(d + o, R)), :], gt_in.at[o],
                      sum_ss.at[o], sum_rs.at[o], dp=lax.rem(d + o, R))

    def all_copy(r, o):
        return remote(gt_all.at[piece(r), :], gt_all.at[piece(r), :],
                      all_ss.at[o], all_rs.at[o], dp=lax.rem(d + o, R))

    gt_own[...] = dot(ctx[...], cg[...], 0, 0)
    gt_out[...] = gt_own[...].astype(BF16)

    @pl.loop(1, R)
    def _(o):
        sum_copy(o).start()

    gctx[...] = dot(cg[...], we[...], 1, 1).astype(BF16)
    store_gctx = pltpu.make_async_copy(gctx, gctx_h, store_sem.at[0])
    store_gctx.start()

    @pl.loop(1, R)
    def _(o):
        sum_copy(o).wait_recv()
        gt_own[piece(d), :] += gt_in[o].astype(F32)

    gt_all[piece(d), :] = gt_own[piece(d), :].astype(BF16)

    @pl.loop(1, R)
    def _(o):
        all_copy(d, o).start()

    @pl.loop(0, CHUNKS)
    def _(ch):
        @pl.loop(1, K)
        def _(o):
            j = 2 * lax.rem(k - o + K, K) + c
            far_copy(j, o, ch).wait_recv()
            fwd_copy(j, o, ch).start()
            acc[rows(ch), :] += dot(codes[j, rows(ch), :], dec[block(j), :], 1, 0)

    @pl.loop(1, R)
    def _(o):
        all_copy(lax.rem(d - o + R, R), o).wait_recv()

    mine = pl.ds(pl.multiple_of(d * own_rows, own_rows), own_rows)
    gw[...] = dot(enc[mine, :], gt_all[...], 1, 1) * (1.0 / R)
    store_gw = pltpu.make_async_copy(gw, gw_h, store_sem.at[1])
    store_gw.start()

    def store_mixed(ch):
        return pltpu.make_async_copy(mixed.at[rows(ch), :], mixed_h.at[rows(ch), :], mix_sem.at[ch])

    @pl.loop(0, CHUNKS)
    def _(ch):
        @pl.loop(1, K)
        def _(o):
            j = 2 * lax.rem(k - o + K, K) + 1 - c
            fwd_copy(j, o, ch).wait_recv()
            acc[rows(ch), :] += dot(codes[j, rows(ch), :], dec[block(j), :], 1, 0)

        mixed[rows(ch), :] = acc[rows(ch), :].astype(BF16)
        store_mixed(ch).start()

    near_copy(t).wait_send()

    @pl.loop(0, CHUNKS)
    def _(ch):
        pair_copy(0, ch).wait_send()

        @pl.loop(1, K)
        def _(o):
            pair_copy(o, ch).wait_send()
            far_copy(t, o, ch).wait_send()
            fwd_copy(2 * lax.rem(k - o + K, K) + c, o, ch).wait_send()

        store_mixed(ch).wait()

    @pl.loop(1, R)
    def _(o):
        sum_copy(o).wait_send()
        all_copy(d, o).wait_send()

    store_gctx.wait()
    store_gw.wait()


def on_device(S, R, context, w_out, encoder, decoder, out_grad):
    T, HW = context.shape
    D, C = encoder.shape
    DL = out_grad.shape[1]
    K = S // 2
    hbm = pl.BlockSpec(memory_space=pl.ANY)
    dma = pltpu.SemaphoreType.DMA
    shapes = [
        ((T, HW), BF16), ((HW, D), BF16), ((D, C), BF16), ((S * C, DL), BF16), ((T, DL), BF16),
        ((HW, C), BF16), ((S, T, C), BF16),
        ((K, T, C), BF16), ((K, T, C), BF16), ((K, T, C), BF16), ((K, T, C), BF16),
        ((T, C), F32), ((T, C), BF16),
        ((HW, C), F32), ((HW, C), BF16), ((R, HW // R, C), BF16), ((HW, C), BF16),
        ((T, DL), F32), ((T, DL), BF16), ((T, HW), BF16), ((D // R, HW), F32),
    ]
    sems = [
        dma((4,)), dma((S,)), dma((2,)), dma((CHUNKS,)),
        dma((K, CHUNKS)), dma((K, CHUNKS)), dma((K, CHUNKS)), dma((K, CHUNKS)),
        dma, dma((K, CHUNKS)), dma((K, CHUNKS)), dma((S, CHUNKS)),
        dma((R,)), dma((R,)), dma((R,)), dma((R,)),
    ]
    return pl.pallas_call(
        functools.partial(kernel, S, R),
        out_shape=(
            jax.ShapeDtypeStruct((T, DL), BF16),
            jax.ShapeDtypeStruct((T, HW), BF16),
            jax.ShapeDtypeStruct((D // R, HW), F32),
        ),
        in_specs=[hbm] * 5,
        out_specs=(hbm,) * 3,
        scratch_shapes=[pltpu.VMEM(s, dt) for s, dt in shapes] + sems,
        compiler_params=pltpu.CompilerParams(
            collective_id=0, has_side_effects=True, vmem_limit_bytes=56 * 1024 * 1024
        ),
        cost_estimate=pl.CostEstimate(flops=6_000_000_000, bytes_accessed=14_000_000, transcendentals=0),
    )(context, w_out, encoder, decoder, out_grad)


def solution(mesh):
    S, R = mesh.shape["tensor"], mesh.shape["dp"]
    in_specs = (P("dp", "tensor"), P("tensor", None), P(), P(None, "tensor"), P("dp", "tensor"))
    out_specs = (P("dp", "tensor"), P("dp", "tensor"), P("dp", "tensor"))
    return jax.shard_map(
        functools.partial(on_device, S, R), mesh=mesh, in_specs=in_specs, out_specs=out_specs, check_vma=False
    )
```

time: 144 us -> 44.2 us (0.31)
  waiting for transfers between devices: 59.8 us -> 0 us
  blocking collectives: 44.1 us -> 0 us
  Pallas kernels: 0 us -> 37.5 us
  matrix products: 23.8 us -> 0 us
  between operations: 14.1 us -> 0.64 us
  local copies, waits for them, and re-layouts: 2.23 us -> 5.8 us
    psum x1 -> x0, blocking collectives: 44.1 us -> none  [on_device(): inner = lax.psum(dot(grad_codes, context, 1, 0), 'dp').astype(jnp.bfloat16)]
    reduce_scatter x1 -> x0, waiting for transfers between devices: 40.9 us -> none  [on_device(): lax.psum_scatter(dot(decoder, out_grad, 1, 1), 'tensor', scatter_dimensio...]
    pallas_call x0 -> x1, Pallas kernels: none -> 37.5 us  [on_device(): pl.pallas_call(functools.partial(kernel, S, R), out_shape=(jax.ShapeDtype...]
    dot_general x7 -> x0, matrix products: 23.8 us -> none  [dot(): lax.dot_general(a, b, (((ca,), (cb,)), ((), ())), preferred_element_type=...]
    all_gather x1 -> x0, waiting for transfers between devices: 18.8 us -> none  [on_device(): lax.all_gather(code, 'tensor', axis=1, tiled=True)]
    unnamed x10 -> x3, local copies, waits for them, and re-layouts: 2.23 us -> 5.8 us
  transfers between devices with their start and end apart: 2 -> 0, of which waited for: 2 -> 0; matrix products, arithmetic and copies ran while one was open for 9% -> 0% of each run, Pallas kernels for 0% -> 0%
where the time goes in v2:
time: 44.2 us; the launch traced here: 43.9 us
  Pallas kernels  37.5 us (85%)
  local copies, waits for them, and re-layouts  5.8 us (13%)
  between operations  0.64 us (1%)
    pallas_call x1, Pallas kernels, on_device(): pl.pallas_call(functools.partial(kernel, S, R), out_shape=(jax.ShapeDtype...  37.5 us
    unnamed x3, local copies, waits for them, and re-layouts  5.8 us

profile of v2, /device:TPU:0, one launch (start us, length us, event | category | flops | bytes accessed | tf_op | source)
XLA Modules:
  0.0 43.9 jit_solution(9546269156783412206)
XLA Ops:
  0.6 37.5 %shard_map.76 = (bf16[512,1024]{1,0:T(8,128)(2,1)}, bf16[512,256]{1,0:T(8,128)(2,1)}, f32[512,256]{1,0:T(8,128)}) custom-call(bf16[512,256]{1,0:T(8,128)(2,1)} %ctx_h.1, bf16[256,4096]{1,0:T(8,128)(2,1)} %w_h.1, bf16[4096,512]{1,0:T(8,128)(2,1)} %enc_h.1, bf16[2048,1024]{1,0:T(8,128)(2,1)} %dec_h.1, bf16[512,1024]{1,0:T(8,128)(2,1)} %og_h.1), custom_call_target="tpu_custom_call" | custom-call | flops 6000000000 | bytes 14000000 | tf_op jit(solution)/shard_map/pallas_call | solution.py:287
  38.1 2.3 %copy.11 = bf16[512,1024]{1,0:T(8,128)(2,1)} copy(bf16[512,1024]{1,0:T(8,128)(2,1)} %get-tuple-element.6) | data formatting | bytes 2097152
  40.4 1.7 %copy.12 = bf16[512,256]{1,0:T(8,128)(2,1)} copy(bf16[512,256]{1,0:T(8,128)(2,1)} %get-tuple-element.7) | data formatting | bytes 524288
  42.1 1.9 %copy.13 = f32[512,256]{1,0:T(8,128)} copy(f32[512,256]{1,0:T(8,128)} %get-tuple-element.8) | data formatting | bytes 1048576

commit v3 on v2

v3 whole, which is shorter than its diff:
```python
import functools

import jax
import jax.numpy as jnp
from jax import lax
from jax.experimental import pallas as pl
from jax.experimental.pallas import tpu as pltpu
from jax.sharding import PartitionSpec as P

BF16, F32 = jnp.bfloat16, jnp.float32
CHUNKS = 2
PARTS = 4


def dot(a, b, ca, cb):
    return lax.dot_general(a, b, (((ca,), (cb,)), ((), ())), preferred_element_type=F32)


def kernel(
    S, R,
    ctx_h, w_h, enc_h, dec_h, og_h,
    mixed_h, gctx_h, gw_h,
    ctx, w, enc, dec, og,
    we, codes, pair_out, pair_in, chip_out, chip_in, cg_own, cg,
    gt_own, gt_out, gt_in, gt_all, acc, mixed, gctx, gw,
    load_sem, dec_sem, store_sem, mix_sem,
    pair_ss, pair_rs, chip_ss, chip_rs, near_ss, far_ss, fwd_ss, code_rs,
    sum_ss, sum_rs, all_ss, all_rs,
):
    K = S // 2
    T, HW = ctx.shape
    C = we.shape[1]
    D = enc.shape[0]
    part = HW // R
    own_rows = D // R
    step = T // CHUNKS
    cut = C // CHUNKS
    d, t = lax.axis_index("dp"), lax.axis_index("tensor")
    k, c = t // 2, lax.rem(t, 2)
    mate = 2 * k + 1 - c

    def chip(o):
        return lax.rem(k + o, K)

    def rows(ch):
        return pl.ds(pl.multiple_of(ch * step, step), step)

    def block(j):
        return pl.ds(pl.multiple_of(j * C, C), C)

    def codes_of(j, ch):
        return pl.ds(pl.multiple_of(j * C + ch * cut, cut), cut)

    def piece(r):
        return pl.ds(pl.multiple_of(r * part, part), part)

    def remote(src, dst, ss, rs, **where):
        return pltpu.make_async_remote_copy(
            src_ref=src, dst_ref=dst, send_sem=ss, recv_sem=rs,
            device_id=where, device_id_type=pl.DeviceIdType.MESH,
        )

    def load(i, src, dst):
        return pltpu.make_async_copy(src, dst, load_sem.at[i])

    def load_dec(j):
        return pltpu.make_async_copy(dec_h.at[block(j), :], dec.at[block(j), :], dec_sem.at[j])

    load_og = load(0, og_h, og)
    load_w, load_enc, load_ctx = load(1, w_h, w), load(2, enc_h, enc), load(3, ctx_h, ctx)
    load_og.start()

    @pl.loop(0, K)
    def _(i):
        o = lax.rem(i + 1, K)
        load_dec(2 * chip(o) + 1 - c).start()
        load_dec(2 * chip(o) + c).start()

    barrier = pltpu.get_barrier_semaphore()
    MESH = pl.DeviceIdType.MESH
    pl.semaphore_signal(barrier, inc=1, device_id={"tensor": mate}, device_id_type=MESH)

    @pl.loop(1, K)
    def _(o):
        pl.semaphore_signal(barrier, inc=1, device_id={"tensor": 2 * chip(o) + c}, device_id_type=MESH)

    @pl.loop(1, R)
    def _(o):
        pl.semaphore_signal(barrier, inc=1, device_id={"dp": lax.rem(d + o, R)}, device_id_type=MESH)

    pl.semaphore_wait(barrier, 1 + (K - 1) + (R - 1))

    def pair_copy(o, ch):
        return remote(pair_out.at[o, ch], pair_in.at[o, ch],
                      pair_ss.at[o, ch], pair_rs.at[o, ch], tensor=mate)

    def chip_copy(o, ch):
        return remote(chip_out.at[o, ch], chip_in.at[o, ch],
                      chip_ss.at[o, ch], chip_rs.at[o, ch], tensor=2 * chip(o) + c)

    load_w.start()
    load_enc.start()
    load_ctx.start()
    load_og.wait()

    def for_mate(o):
        j = 2 * chip(o) + 1 - c
        load_dec(j).wait()

        @pl.loop(0, CHUNKS)
        def _(ch):
            pair_out[o, ch] = dot(og[...], dec[codes_of(j, ch), :], 1, 1).astype(BF16)
            pair_copy(o, ch).start()

    @pl.loop(1, K)
    def _(o):
        for_mate(o)
        j = 2 * chip(o) + c
        load_dec(j).wait()

        @pl.loop(0, CHUNKS)
        def _(ch):
            cg_own[ch] = dot(og[...], dec[codes_of(j, ch), :], 1, 1)
            pair_copy(o, ch).wait_recv()
            chip_out[o, ch] = (cg_own[ch] + pair_in[o, ch].astype(F32)).astype(BF16)
            chip_copy(o, ch).start()

    for_mate(0)
    load_dec(t).wait()

    @pl.loop(0, CHUNKS)
    def _(ch):
        cg_own[ch] = dot(og[...], dec[codes_of(t, ch), :], 1, 1)

    load_w.wait()
    load_enc.wait()
    we[...] = dot(w[...], enc[...], 1, 0).astype(BF16)
    load_ctx.wait()

    def near_copy(j):
        return remote(codes.at[j], codes.at[j], near_ss, code_rs.at[j, 0], tensor=mate)

    def far_copy(j, o, ch):
        return remote(codes.at[j, rows(ch), :], codes.at[j, rows(ch), :],
                      far_ss.at[o, ch], code_rs.at[j, ch], tensor=2 * chip(o) + c)

    def fwd_copy(j, o, ch):
        return remote(codes.at[j, rows(ch), :], codes.at[j, rows(ch), :],
                      fwd_ss.at[o, ch], code_rs.at[j, ch], tensor=mate)

    codes[t] = dot(ctx[...], we[...], 1, 0).astype(BF16)
    near_copy(t).start()

    def sum_copy(o, ch):
        return remote(gt_out.at[ch, piece(lax.rem(d + o, R)), :], gt_in.at[ch, o],
                      sum_ss.at[o, ch], sum_rs.at[o, ch], dp=lax.rem(d + o, R))

    def all_copy(r, o, ch):
        return remote(gt_all.at[ch, piece(r), :], gt_all.at[ch, piece(r), :],
                      all_ss.at[o, ch], all_rs.at[o, ch], dp=lax.rem(d + o, R))

    for ch in range(CHUNKS):
        pair_copy(0, ch).wait_recv()
        cg_own[ch] += pair_in[0, ch].astype(F32)

        @pl.loop(1, K)
        def _(o):
            chip_copy(o, ch).wait_recv()
            cg_own[ch] += chip_in[o, ch].astype(F32)

        if ch == CHUNKS - 1:
            @pl.loop(1, K)
            def _(o):
                @pl.loop(0, CHUNKS)
                def _(part_of):
                    chip_copy(o, part_of).wait_send()
                    far_copy(t, o, part_of).start()

        cg[ch] = cg_own[ch].astype(BF16)
        gt_own[ch] = dot(ctx[...], cg[ch], 0, 0)
        gt_out[ch] = gt_own[ch].astype(BF16)

        @pl.loop(1, R)
        def _(o):
            sum_copy(o, ch).start()

    def total(ch):
        @pl.loop(1, R)
        def _(o):
            sum_copy(o, ch).wait_recv()
            gt_own[ch, piece(d), :] += gt_in[ch, o].astype(F32)

        gt_all[ch, piece(d), :] = gt_own[ch, piece(d), :].astype(BF16)

        @pl.loop(1, R)
        def _(o):
            all_copy(d, o, ch).start()

    @pl.loop(0, CHUNKS)
    def _(ch):
        acc[rows(ch), :] = dot(codes[t, rows(ch), :], dec[block(t), :], 1, 0)

    near_copy(mate).wait_recv()

    @pl.loop(0, CHUNKS)
    def _(ch):
        acc[rows(ch), :] += dot(codes[mate, rows(ch), :], dec[block(mate), :], 1, 0)

    total(0)
    gctx[...] = sum(
        dot(cg[ch], we[:, ch * cut:(ch + 1) * cut], 1, 1) for ch in range(CHUNKS)
    ).astype(BF16)
    store_gctx = pltpu.make_async_copy(gctx, gctx_h, store_sem.at[0])
    store_gctx.start()
    for ch in range(1, CHUNKS):
        total(ch)

    @pl.loop(0, CHUNKS)
    def _(ch):
        @pl.loop(1, K)
        def _(o):
            j = 2 * lax.rem(k - o + K, K) + c
            far_copy(j, o, ch).wait_recv()
            fwd_copy(j, o, ch).start()
            acc[rows(ch), :] += dot(codes[j, rows(ch), :], dec[block(j), :], 1, 0)

    mine = pl.ds(pl.multiple_of(d * own_rows, own_rows), own_rows)
    for ch in range(CHUNKS):
        @pl.loop(1, R)
        def _(o):
            all_copy(lax.rem(d - o + R, R), o, ch).wait_recv()

        term = dot(enc[mine, ch * cut:(ch + 1) * cut], gt_all[ch], 1, 1) * (1.0 / R)
        gw[...] = term if ch == 0 else gw[...] + term

    store_gw = pltpu.make_async_copy(gw, gw_h, store_sem.at[1])
    store_gw.start()

    def store_mixed(ch):
        return pltpu.make_async_copy(mixed.at[rows(ch), :], mixed_h.at[rows(ch), :], mix_sem.at[ch])

    @pl.loop(0, CHUNKS)
    def _(ch):
        @pl.loop(1, K)
        def _(o):
            j = 2 * lax.rem(k - o + K, K) + 1 - c
            fwd_copy(j, o, ch).wait_recv()
            acc[rows(ch), :] += dot(codes[j, rows(ch), :], dec[block(j), :], 1, 0)

        mixed[rows(ch), :] = acc[rows(ch), :].astype(BF16)
        store_mixed(ch).start()

    near_copy(t).wait_send()

    @pl.loop(0, CHUNKS)
    def _(ch):
        pair_copy(0, ch).wait_send()

        @pl.loop(1, K)
        def _(o):
            pair_copy(o, ch).wait_send()
            far_copy(t, o, ch).wait_send()
            fwd_copy(2 * lax.rem(k - o + K, K) + c, o, ch).wait_send()

        store_mixed(ch).wait()

    @pl.loop(1, R)
    def _(o):
        for ch in range(CHUNKS):
            sum_copy(o, ch).wait_send()
            all_copy(d, o, ch).wait_send()

    store_gctx.wait()
    store_gw.wait()


def hand_over(a, b, c, x, y, z):
    x[...], y[...], z[...] = a[...], b[...], c[...]


def on_device(S, R, context, w_out, encoder, decoder, out_grad):
    T, HW = context.shape
    D, C = encoder.shape
    DL = out_grad.shape[1]
    K, N = S // 2, CHUNKS
    hbm = pl.BlockSpec(memory_space=pl.ANY)
    dma = pltpu.SemaphoreType.DMA
    shapes = [
        ((T, HW), BF16), ((HW, D), BF16), ((D, C), BF16), ((S * C, DL), BF16), ((T, DL), BF16),
        ((HW, C), BF16), ((S, T, C), BF16),
        ((K, N, T, C // N), BF16), ((K, N, T, C // N), BF16),
        ((K, N, T, C // N), BF16), ((K, N, T, C // N), BF16),
        ((N, T, C // N), F32), ((N, T, C // N), BF16),
        ((N, HW, C // N), F32), ((N, HW, C // N), BF16),
        ((N, R, HW // R, C // N), BF16), ((N, HW, C // N), BF16),
        ((T, DL), F32), ((T, DL), BF16), ((T, HW), BF16), ((D // R, HW), F32),
    ]
    sems = [
        dma((4,)), dma((S,)), dma((2,)), dma((CHUNKS,)),
        dma((K, CHUNKS)), dma((K, CHUNKS)), dma((K, CHUNKS)), dma((K, CHUNKS)),
        dma, dma((K, CHUNKS)), dma((K, CHUNKS)), dma((S, CHUNKS)),
        dma((R, N)), dma((R, N)), dma((R, N)), dma((R, N)),
    ]
    out_shape = (
        jax.ShapeDtypeStruct((T, DL), BF16),
        jax.ShapeDtypeStruct((T, HW), BF16),
        jax.ShapeDtypeStruct((D // R, HW), F32),
    )
    results = pl.pallas_call(
        functools.partial(kernel, S, R),
        out_shape=out_shape,
        in_specs=[hbm] * 5,
        out_specs=(hbm,) * 3,
        scratch_shapes=[pltpu.VMEM(s, dt) for s, dt in shapes] + sems,
        compiler_params=pltpu.CompilerParams(
            collective_id=0, has_side_effects=True, vmem_limit_bytes=56 * 1024 * 1024
        ),
        cost_estimate=pl.CostEstimate(flops=6_000_000_000, bytes_accessed=14_000_000, transcendentals=0),
    )(context, w_out, encoder, decoder, out_grad)
    return pl.pallas_call(
        hand_over,
        out_shape=out_shape,
        grid=(PARTS,),
        in_specs=[pl.BlockSpec((s.shape[0] // PARTS, s.shape[1]), lambda i: (i, 0)) for s in out_shape],
        out_specs=tuple(pl.BlockSpec((s.shape[0] // PARTS, s.shape[1]), lambda i: (i, 0)) for s in out_shape),
        cost_estimate=pl.CostEstimate(flops=0, bytes_accessed=4_000_000, transcendentals=0),
    )(*results)


def solution(mesh):
    S, R = mesh.shape["tensor"], mesh.shape["dp"]
    in_specs = (P("dp", "tensor"), P("tensor", None), P(), P(None, "tensor"), P("dp", "tensor"))
    out_specs = (P("dp", "tensor"), P("dp", "tensor"), P("dp", "tensor"))
    return jax.shard_map(
        functools.partial(on_device, S, R), mesh=mesh, in_specs=in_specs, out_specs=out_specs, check_vma=False
    )
```

time: 44.2 us -> 42.8 us (0.968)
  local copies, waits for them, and re-layouts: 5.8 us -> 0 us
  Pallas kernels: 37.5 us -> 42 us
    unnamed x3 -> x0, local copies, waits for them, and re-layouts: 5.8 us -> none
    pallas_call x1 -> x2, Pallas kernels: 37.5 us -> 42 us  [the longest x1 38.3 us: on_device(): pl.pallas_call(functools.partial(kernel, S, R), out_shape=out_shape, in_s...]
where the time goes in v3:
time: 42.8 us; the launch traced here: 42.6 us
  Pallas kernels  42 us (98%)
  between operations  0.64 us (1%)
    pallas_call x1, Pallas kernels, on_device(): pl.pallas_call(functools.partial(kernel, S, R), out_shape=out_shape, in_s...  38.3 us
    pallas_call x1, Pallas kernels, on_device(): pl.pallas_call(hand_over, out_shape=out_shape, grid=(PARTS,), in_specs=[p...  3.68 us

profile of v3, /device:TPU:0, one launch (start us, length us, event | category | flops | bytes accessed | tf_op | source)
XLA Modules:
  0.0 42.6 jit_solution(17563601566798512309)
XLA Ops:
  0.6 38.3 %shard_map.76 = (bf16[512,1024]{1,0:T(8,128)(2,1)}, bf16[512,256]{1,0:T(8,128)(2,1)}, f32[512,256]{1,0:T(8,128)}) custom-call(bf16[512,256]{1,0:T(8,128)(2,1)} %ctx_h.1, bf16[256,4096]{1,0:T(8,128)(2,1)} %w_h.1, bf16[4096,512]{1,0:T(8,128)(2,1)} %enc_h.1, bf16[2048,1024]{1,0:T(8,128)(2,1)} %dec_h.1, bf16[512,1024]{1,0:T(8,128)(2,1)} %og_h.1), custom_call_target="tpu_custom_call" | custom-call | flops 6000000000 | bytes 14000000 | tf_op jit(solution)/shard_map/pallas_call | solution.py:309
  38.9 3.7 %shard_map.77 = (bf16[512,1024]{1,0:T(8,128)(2,1)}, bf16[512,256]{1,0:T(8,128)(2,1)}, f32[512,256]{1,0:T(8,128)}) custom-call(bf16[512,1024]{1,0:T(8,128)(2,1)} %get-tuple-element.6.a, bf16[512,256]{1,0:T(8,128)(2,1)} %get-tuple-element.7.b, f32[512,256]{1,0:T(8,128)} %get-tuple-element.8.c), custom_call_target="tpu_custom_call" | custom-call | bytes 4000000 | tf_op jit(solution)/shard_map/pallas_call | solution.py:320
